TPU v7x, 32 devices: a whole 2x2x4 slice. The times are simulated.
32 devices in a mesh: gr: 8 (over y, x, core), gc: 4 (over z).
Axes of the slice: x: 2, y: 2, z: 4, core: 2. Of those that a mesh axis runs over, the one named last changes fastest.
Arguments:
- border: bfloat16 [24, 768, 2048], P('gc', None, 'gr'), may hold values from -1 to 1
- row_scale: float32 [24, 768], P('gc'), may hold values from 0.1 to 10
- block_pick: int32 [24, 16], replicated, may hold values from 0 to 3
- given_diag: float32 [8192], replicated, may hold values from 0.5 to 4
Outputs:
- factored: float32 [8192, 8192], P('gr', 'gc')
All inputs are finite; a program needn't handle non-finite values.
Results may differ from a plain program's by a relative error of at most 0.00097.
Values may be sent and summed in bfloat16 or wider, within the bound.
A program may use at most 128 MiB of HBM per device.

v0:
```python
import functools

import jax
import jax.numpy as jnp
from jax import lax
from jax.experimental import pallas as pl
from jax.experimental.pallas import tpu as pltpu
from jax.sharding import PartitionSpec as P

N = 8192
BLK = 128
NWIN = 16
WSPAN = 4
HEAD = 512
MESH = pl.DeviceIdType.MESH


def ring_swap(p):
    return p + ((p // 2) % 2) * (1 - 2 * (p % 2))


def gather_kernel(dims, scaled, rows, cols, head, own_sem, zrecv, zsend, recv, rsend, ssend):
    grid_rows, grid_cols, roots, parts, group = dims
    chips = grid_rows // 2
    units = grid_cols * parts
    me = lax.axis_index("gr")
    z = lax.axis_index("gc")
    core = lax.rem(me, 2)
    pos = ring_swap(me // 2)
    sibling = me + 1 - 2 * core
    ahead = ring_swap(lax.rem(pos + 1, chips)) * 2 + core
    behind = ring_swap(lax.rem(pos + chips - 1, chips)) * 2 + core
    has_up = z < grid_cols - 1
    has_down = z > 0

    barrier = pltpu.get_barrier_semaphore()
    for other in (sibling, ahead, behind):
        pl.semaphore_signal(barrier, inc=1, device_id=(other, z), device_id_type=MESH)

    @pl.when(has_up)
    def _():
        pl.semaphore_signal(barrier, inc=1, device_id=(me, z + 1), device_id_type=MESH)

    @pl.when(has_down)
    def _():
        pl.semaphore_signal(barrier, inc=1, device_id=(me, z - 1), device_id_type=MESH)

    own = pltpu.make_async_copy(
        scaled, rows.at[pl.ds(z * parts * group, parts * group)], own_sem
    )
    own.start()
    pl.semaphore_wait(barrier, 3 + has_up.astype(jnp.int32) + has_down.astype(jnp.int32))
    def mine(s):
        return scaled.at[pl.ds(s * group, group)]

    def zcopy(unit, up, src=None):
        where = pl.ds(unit * group, group)
        return pltpu.make_async_remote_copy(
            src_ref=rows.at[where] if src is None else src,
            dst_ref=rows.at[where],
            send_sem=zsend.at[1 if up else 0, unit],
            recv_sem=zrecv.at[unit],
            device_id=(me, z + 1 if up else z - 1),
            device_id_type=MESH,
        )

    def target(k, unit):
        where = pl.ds(unit * group, group)
        return head.at[where] if k == roots else cols.at[k, where]

    def narrow(k, ref):
        return ref.at[:, :, pl.ds(0, BLK)] if k == roots else ref

    def ring_copy(k, unit, src, forward):
        return pltpu.make_async_remote_copy(
            src_ref=src,
            dst_ref=target(k, unit),
            send_sem=rsend.at[k, unit],
            recv_sem=recv.at[k, unit],
            device_id=(ahead if forward else behind, z),
            device_id_type=MESH,
        )

    def sibling_copy(k, unit, src):
        return pltpu.make_async_remote_copy(
            src_ref=src,
            dst_ref=target(k, unit),
            send_sem=ssend.at[k, unit],
            recv_sem=recv.at[k, unit],
            device_id=(sibling, z),
            device_id_type=MESH,
        )

    def stream(k):
        root = z * roots + k if k < roots else 0 * z
        on_ring = core == lax.rem(root, 2)
        d = lax.rem(pos - ring_swap(root // 2) + chips, chips)
        return on_ring, d, lax.rem(chips - d, chips)

    streams = [stream(k) for k in range(roots + 1)]

    def send_along(k, unit, hop, forward, own_part):
        def both(src):
            ring_copy(k, unit, src, forward).start()
            sibling_copy(k, unit, src).start()

        @pl.when(hop == 0)
        def _():
            here = unit // parts == z

            @pl.when(here)
            def _():
                both(narrow(k, mine(own_part)))

            @pl.when(jnp.logical_not(here))
            def _():
                both(narrow(k, rows.at[pl.ds(unit * group, group)]))

        @pl.when(hop > 0)
        def _():
            ring_copy(k, unit, target(k, unit), forward).wait_recv()

            @pl.when(hop < chips - 1)
            def _():
                ring_copy(k, unit, target(k, unit), forward).start()

            sibling_copy(k, unit, target(k, unit)).start()

    def step(i, carry):
        t, s = i // parts, lax.rem(i, parts)
        low, high = z - t, z + t

        @pl.when(t == 0)
        def _():
            @pl.when(has_up)
            def _():
                zcopy(z * parts + s, True, mine(s)).start()

            @pl.when(has_down)
            def _():
                zcopy(z * parts + s, False, mine(s)).start()

        later = jnp.logical_and(t > 0, t < grid_cols)

        @pl.when(jnp.logical_and(later, low >= 0))
        def _():
            zcopy(low * parts + s, True).wait_recv()

            @pl.when(has_up)
            def _():
                zcopy(low * parts + s, True).start()

        @pl.when(jnp.logical_and(later, high < grid_cols))
        def _():
            zcopy(high * parts + s, False).wait_recv()

            @pl.when(has_down)
            def _():
                zcopy(high * parts + s, False).start()

        for forward in (True, False):
            for k in range(roots + 1):
                on_ring, d_ahead, d_behind = streams[k]
                hop = d_ahead if forward else d_behind
                slot = i - hop
                t2, s2 = slot // parts, lax.rem(slot, parts)
                good = jnp.logical_and(slot >= 0, slot < units)
                good = jnp.logical_and(good, lax.rem(slot, 2) == (0 if forward else 1))
                good = jnp.logical_and(good, on_ring)

                @pl.when(jnp.logical_and(good, z - t2 >= 0))
                def _():
                    send_along(k, (z - t2) * parts + s2, hop, forward, s2)

                other = jnp.logical_and(t2 > 0, z + t2 < grid_cols)

                @pl.when(jnp.logical_and(good, other))
                def _():
                    send_along(k, (z + t2) * parts + s2, hop, forward, s2)

        return carry

    lax.fori_loop(0, units + chips - 1, step, 0)

    def finish(unit, carry):
        c, s = unit // parts, lax.rem(unit, parts)

        @pl.when(jnp.logical_and(c <= z, has_up))
        def _():
            zcopy(unit, True).wait_send()

        @pl.when(jnp.logical_and(c >= z, has_down))
        def _():
            zcopy(unit, False).wait_send()

        slot = jnp.where(c > z, c - z, z - c) * parts + s
        even = lax.rem(slot, 2) == 0
        for k in range(roots + 1):
            on_ring, d_ahead, d_behind = streams[k]
            hop = jnp.where(even, d_ahead, d_behind)

            @pl.when(on_ring)
            def _():
                @pl.when(hop < chips - 1)
                def _():
                    ring_copy(k, unit, target(k, unit), True).wait_send()

                sibling_copy(k, unit, target(k, unit)).wait_send()

            @pl.when(jnp.logical_not(on_ring))
            def _():
                sibling_copy(k, unit, target(k, unit)).wait_recv()

        return carry

    lax.fori_loop(0, units, finish, 0)
    own.wait()


def gather(scaled, grid_rows, grid_cols):
    here, depth, width = scaled.shape
    roots = grid_rows // grid_cols
    parts = here if grid_cols <= 4 else 1
    group = here // parts
    units = grid_cols * parts
    total = here * grid_cols
    dims = (grid_rows, grid_cols, roots, parts, group)
    dma = pltpu.SemaphoreType.DMA
    return pl.pallas_call(
        functools.partial(gather_kernel, dims),
        out_shape=(
            jax.ShapeDtypeStruct((total, depth, width), scaled.dtype),
            jax.ShapeDtypeStruct((roots, total, depth, width), scaled.dtype),
            jax.ShapeDtypeStruct((total, depth, BLK), scaled.dtype),
        ),
        in_specs=[pl.BlockSpec(memory_space=pl.ANY)],
        out_specs=[pl.BlockSpec(memory_space=pl.ANY)] * 3,
        scratch_shapes=[
            dma,
            dma((units,)),
            dma((2, units)),
            dma((roots + 1, units)),
            dma((roots + 1, units)),
            dma((roots + 1, units)),
        ],
        compiler_params=pltpu.CompilerParams(collective_id=0, has_side_effects=True),
        name="gather",
    )(scaled)


def full_dot(a, b, dims):
    return lax.dot_general(
        a, b, (dims, ((), ())), precision=lax.Precision.HIGHEST, preferred_element_type=jnp.float32
    )


def split(x):
    high = x.astype(jnp.bfloat16)
    return high, (x - high.astype(jnp.float32)).astype(jnp.bfloat16)


def three_dot(a, b, dims):
    dot = functools.partial(
        lax.dot_general, dimension_numbers=(dims, ((), ())), preferred_element_type=jnp.float32
    )
    return dot(a[0], b[0]) + (dot(a[0], b[1]) + dot(a[1], b[0]))


STEP = 4


def eliminate(jj, aug):
    rb = lax.broadcasted_iota(jnp.int32, (BLK, BLK), 0)
    cb = lax.broadcasted_iota(jnp.int32, (BLK, BLK), 1)
    lane = lax.broadcasted_iota(jnp.int32, (1, BLK), 1)
    j = jj * STEP
    block = aug[...]
    rows = [aug[pl.ds(j + a, 1), :] for a in range(STEP)]
    pick = lambda x, at, n: jnp.sum(jnp.where(at == n, x, 0.0), axis=1, keepdims=True)
    cols = [pick(block[:, :BLK], cb, j + a) for a in range(STEP)]
    low = [[None] * STEP for _ in range(STEP)]
    inv = [None] * STEP
    for a in range(STEP):
        for b in range(a + 1):
            v = pick(rows[b][:, :BLK], lane, j + a)
            for c in range(b):
                v = v - low[b][c] * low[a][c]
            if a == b:
                inv[a] = lax.rsqrt(v)
            else:
                low[a][b] = v * inv[b]
    done = rb[:, :1]
    units, factors = [], []
    for a in range(STEP):
        u, f = rows[a], cols[a]
        for b in range(a):
            u = u - low[a][b] * units[b]
            f = f - low[a][b] * factors[b]
        units.append(u * inv[a])
        factors.append(f * inv[a])
    for a in range(STEP):
        block = block - jnp.where(done >= j + STEP, factors[a], 0.0) * units[a]
    aug[...] = block
    for a in range(STEP):
        aug[pl.ds(j + a, 1), :] = units[a]


def factor(work, lower, inverse, aug):
    blocks = HEAD // BLK
    lower[...] = jnp.zeros_like(lower)
    inverse[...] = jnp.zeros_like(inverse)
    rb = lax.broadcasted_iota(jnp.int32, (BLK, BLK), 0)
    cb = lax.broadcasted_iota(jnp.int32, (BLK, BLK), 1)
    for kb in range(blocks):
        lo, hi = kb * BLK, (kb + 1) * BLK
        aug[:, :BLK] = work[lo:hi, lo:hi]
        aug[:, BLK:] = jnp.where(rb == cb, 1.0, 0.0)

        def turn(jj, carry):
            eliminate(jj, aug)
            return carry

        lax.fori_loop(0, BLK // STEP, turn, 0)
        upper = jnp.where(cb >= rb, aug[:, :BLK], 0.0)
        inv = jnp.where(cb <= rb, aug[:, BLK:], 0.0)
        lower[lo:hi, lo:hi] = upper.T
        inverse[lo:hi, lo:hi] = inv
        if hi < HEAD:
            below = full_dot(work[hi:, lo:hi], inv, ((1,), (1,)))
            lower[hi:, lo:hi] = below
            work[hi:, hi:] = work[hi:, hi:] - full_dot(below, below, ((1,), (1,)))
        if kb > 0:
            mix = full_dot(lower[lo:hi, :lo], inverse[:lo, :lo], ((1,), (0,)))
            inverse[lo:hi, :lo] = -full_dot(inv, mix, ((1,), (0,)))


def finish_kernel(
    roots, place, row_pick, col_pick, head_pick, rows, cols, head, diag_head, diag_cols, out,
    left, top, corner, lower, inverse, aug, lhs, rhs, top_high, top_low,
):
    s = pl.program_id(0)
    row_zero, col_zero, own_stream, own_head = place[0], place[1], place[2], place[3]
    width = rows.shape[2]
    row_wins = width // BLK

    @pl.when(s == 0)
    def _():
        out[...] = jnp.zeros_like(out)
        left[...] = jnp.zeros_like(left)
        top[...] = jnp.zeros_like(top)
        r = lax.broadcasted_iota(jnp.int32, (HEAD, HEAD), 0)
        c = lax.broadcasted_iota(jnp.int32, (HEAD, HEAD), 1)
        corner[...] = jnp.where(r == c, diag_head[...], 0.0)

    lhs[:, :width] = rows[0]
    for k in range(roots):
        part = slice(k * width, (k + 1) * width)

        @pl.when(own_stream == k)
        def _():
            rhs[:, part] = rows[0]

        @pl.when(own_stream != k)
        def _():
            rhs[:, part] = cols[k, 0]

    @pl.when(own_head == 1)
    def _():
        lhs[:, width:] = rows[0, :, :BLK]
        rhs[:, roots * width :] = rows[0, :, :BLK]

    @pl.when(own_head == 0)
    def _():
        lhs[:, width:] = head[0]
        rhs[:, roots * width :] = head[0]

    gram = lax.dot_general(
        lhs[...], rhs[...], (((0,), (0,)), ((), ())), preferred_element_type=jnp.float32
    )

    def spot(win, pick):
        return pl.ds(pl.multiple_of(win * WSPAN * BLK + pick * BLK, BLK), BLK)

    at_head = spot(0, head_pick[s])
    cut = lambda a, b: gram[a * BLK : (a + 1) * BLK, b * BLK : (b + 1) * BLK]
    col_wins = roots * row_wins
    corner[at_head, at_head] += cut(row_wins, col_wins)
    for a in range(row_wins):
        left[spot(a, row_pick[s, a]), at_head] += cut(a, col_wins)
    for b in range(col_wins):
        here = spot(b, col_pick[s, b])
        top[at_head, here] += cut(row_wins, b)
        for a in range(row_wins):
            out[spot(a, row_pick[s, a]), here] += cut(a, b)

    @pl.when(s == pl.num_programs(0) - 1)
    def _():
        factor(corner, lower, inverse, aug)
        inv = split(inverse[...])
        n_rows, n_cols = out.shape
        wide = 512
        for c in range(n_cols // wide):
            at = slice(c * wide, (c + 1) * wide)
            top_high[:, at], top_low[:, at] = split(
                three_dot(inv, split(top[:, at]), ((1,), (0,)))
            )
        tile = 256

        def strip(i, carry):
            at = pl.ds(pl.multiple_of(i * tile, tile), tile)
            panel = three_dot(split(left[at, :]), inv, ((1,), (1,)))
            first = row_zero + i * tile

            @pl.when(first >= HEAD)
            def _():
                product = three_dot(split(panel), (top_high[...], top_low[...]), ((1,), (0,)))
                r = first + lax.broadcasted_iota(jnp.int32, (tile, n_cols), 0)
                c = col_zero + lax.broadcasted_iota(jnp.int32, (tile, n_cols), 1)
                out[at, :] = out[at, :] + jnp.where(r == c, diag_cols[...], 0.0) - product

                @pl.when(col_zero == 0)
                def _():
                    out[at, :HEAD] = panel

            @pl.when(first < HEAD)
            def _():
                out[at, :] = jnp.zeros((tile, n_cols), jnp.float32)

                @pl.when(col_zero == 0)
                def _():
                    out[at, :HEAD] = lower[pl.ds(pl.multiple_of(first, tile), tile), :]

            return carry

        lax.fori_loop(0, n_rows // tile, strip, 0)


def finish(place, row_pick, col_pick, head_pick, rows, cols, head, diag_head, diag_cols, n_rows, n_cols):
    total, depth, width = rows.shape
    roots = cols.shape[0]
    f32, bf16 = jnp.float32, jnp.bfloat16
    whole = lambda s, *_: (0, 0)
    grid_spec = pltpu.PrefetchScalarGridSpec(
        num_scalar_prefetch=4,
        grid=(total,),
        in_specs=[
            pl.BlockSpec((1, depth, width), lambda s, *_: (s, 0, 0)),
            pl.BlockSpec((roots, 1, depth, width), lambda s, *_: (0, s, 0, 0)),
            pl.BlockSpec((1, depth, BLK), lambda s, *_: (s, 0, 0)),
            pl.BlockSpec((1, HEAD), whole),
            pl.BlockSpec((1, n_cols), whole),
        ],
        out_specs=pl.BlockSpec((n_rows, n_cols), whole),
        scratch_shapes=[
            pltpu.VMEM((n_rows, HEAD), f32),
            pltpu.VMEM((HEAD, n_cols), f32),
            pltpu.VMEM((HEAD, HEAD), f32),
            pltpu.VMEM((HEAD, HEAD), f32),
            pltpu.VMEM((HEAD, HEAD), f32),
            pltpu.VMEM((BLK, 2 * BLK), f32),
            pltpu.VMEM((depth, width + BLK), bf16),
            pltpu.VMEM((depth, roots * width + BLK), bf16),
            pltpu.VMEM((HEAD, n_cols), bf16),
            pltpu.VMEM((HEAD, n_cols), bf16),
        ],
    )
    return pl.pallas_call(
        functools.partial(finish_kernel, roots),
        grid_spec=grid_spec,
        out_shape=jax.ShapeDtypeStruct((n_rows, n_cols), f32),
        compiler_params=pltpu.CompilerParams(vmem_limit_bytes=56 * 1024 * 1024),
        name="finish",
    )(
        place, row_pick, col_pick, head_pick, rows, cols, head,
        diag_head.reshape(1, HEAD), diag_cols.reshape(1, n_cols),
    )


def body(border, row_scale, block_pick, given_diag):
    grid_rows = lax.axis_size("gr")
    grid_cols = lax.axis_size("gc")
    row_index = lax.axis_index("gr")
    col_index = lax.axis_index("gc")
    row_windows = NWIN // grid_rows
    col_windows = NWIN // grid_cols
    local_rows = N // grid_rows
    local_cols = N // grid_cols
    scaled = (jnp.sqrt(row_scale)[:, :, None] * border.astype(jnp.float32)).astype(jnp.bfloat16)
    rows, cols, head = gather(scaled, grid_rows, grid_cols)
    row_pick = lax.dynamic_slice_in_dim(block_pick, row_index * row_windows, row_windows, 1)
    col_pick = lax.dynamic_slice_in_dim(block_pick, col_index * col_windows, col_windows, 1)
    roots = grid_rows // grid_cols
    own_stream = row_index - col_index * roots
    place = jnp.stack(
        [
            row_index * local_rows,
            col_index * local_cols,
            own_stream,
            (row_index == 0).astype(jnp.int32),
        ]
    ).astype(jnp.int32)
    diag_cols = lax.dynamic_slice_in_dim(given_diag, col_index * local_cols, local_cols, 0)
    return finish(
        place, row_pick, col_pick, block_pick[:, 0], rows, cols, head,
        given_diag[:HEAD], diag_cols, local_rows, local_cols,
    )


def solution(mesh):
    in_specs = (P("gc", None, "gr"), P("gc", None), P(), P())
    out_specs = P("gr", "gc")
    return jax.shard_map(body, mesh=mesh, in_specs=in_specs, out_specs=out_specs, check_vma=False)
```

profile of v0, /device:TPU:29, one launch (start us, length us, event | category | flops | bytes accessed | tf_op | source)
XLA Modules:
  0.0 288.7 jit_solution(14673555756946012446)
XLA Ops:
  0.0 0.6 pad_add_fusion.place
  0.6 0.7 constant_dynamic-slice_fusion.1
  1.3 1.2 slice_bitcast_fusion.head_pick
  2.5 0.7 constant_dynamic-slice_fusion
  3.2 1.3 slice.7
  4.5 1.3 dynamic_slice.11
  5.7 0.7 copy.8.col_pick
  6.4 0.7 copy.7.row_pick
  7.1 0.7 sqrt.3
  7.9 3.1 %multiply_convert_fusion.scaled = bf16[6,768,256]{2,1,0:T(8,128)(2,1)} fusion(bf16[6,768,256]{2,1,0:T(8,128)(2,1)} %param.4, f32[6,768]{1,0:T(8,128)S(1)} %sqrt.3), kind=kLoop, calls=%fused_computation | loop fusion | flops 3538944 | bytes 4737024 | tf_op jit(solution)/shard_map/convert_element_type | solution.py:488
  10.9 202.3 %gather.1 = (bf16[24,768,256]{2,1,0:T(8,128)(2,1)}, bf16[2,24,768,256]{3,2,1,0:T(8,128)(2,1)}, bf16[24,768,128]{2,1,0:T(8,128)(2,1)}) custom-call(bf16[6,768,256]{2,1,0:T(8,128)(2,1)} %multiply_convert_fusion.scaled), custom_call_target="tpu_custom_call" | custom-call | tf_op jit(solution)/shard_map/gather/pallas_call | solution.py:229
  213.2 75.5 %finish.1 = f32[1024,2048]{1,0:T(8,128)} custom-call(s32[4]{0:T(128)} %pad_add_fusion.place, s32[24,2]{1,0:T(8,128)} %copy.7.row_pick, s32[24,4]{1,0:T(8,128)} %copy.8.col_pick, s32[24]{0:T(128)} %slice_bitcast_fusion.head_pick, bf16[24,768,256]{2,1,0:T(8,128)(2,1)} %get-tuple-element.8.rows, bf16[2,24,768,256]{3,2,1,0:T(8,128)(2,1)} %get-tuple-element.9.cols, ...), custom_call_target="tpu_custom_call" | custom-call | tf_op jit(solution)/shard_map/finish/pallas_call | solution.py:467
where the time goes:
time: 290 us; the launch traced here: 289 us
  Pallas kernels  278 us (96%)
  local copies, waits for them, and re-layouts  7.25 us (2%)
  other arithmetic  3.67 us (1%)
    pallas_call x1, Pallas kernels, gather(): pl.pallas_call(functools.partial(gather_kernel, dims), out_shape=(jax.Sha...  202 us
    pallas_call x1, Pallas kernels, finish(): pl.pallas_call(functools.partial(finish_kernel, roots), grid_spec=grid_sp...  75.5 us

commit v1 on v0

--- a/solution.py
+++ b/solution.py
@@ -13,6 +13,7 @@
 WSPAN = 4
 HEAD = 512
 MESH = pl.DeviceIdType.MESH
+PIECES = 2
 
 
 def ring_swap(p):
@@ -486,7 +487,14 @@
     local_rows = N // grid_rows
     local_cols = N // grid_cols
     scaled = (jnp.sqrt(row_scale)[:, :, None] * border.astype(jnp.float32)).astype(jnp.bfloat16)
-    rows, cols, head = gather(scaled, grid_rows, grid_cols)
+    here, depth, width = scaled.shape
+    pieces = PIECES if grid_cols <= 4 else 1
+    rows, cols, head = gather(
+        scaled.reshape(here * pieces, depth // pieces, width), grid_rows, grid_cols
+    )
+    rows = rows.reshape(-1, depth, width)
+    cols = cols.reshape(-1, rows.shape[0], depth, width)
+    head = head.reshape(-1, depth, BLK)
     row_pick = lax.dynamic_slice_in_dim(block_pick, row_index * row_windows, row_windows, 1)
     col_pick = lax.dynamic_slice_in_dim(block_pick, col_index * col_windows, col_windows, 1)
     roots = grid_rows // grid_cols

time: 290 us -> 330 us (1.14)
  Pallas kernels: 278 us -> 318 us
    pallas_call x1, Pallas kernels: 202 us -> 242 us  [gather(): pl.pallas_call(functools.partial(gather_kernel, dims), out_shape=(jax.Sha...]
where the time goes in v1:
time: 330 us; the launch traced here: 329 us
  Pallas kernels  318 us (96%)
  local copies, waits for them, and re-layouts  7.25 us (2%)
  other arithmetic  3.67 us (1%)
    pallas_call x1, Pallas kernels, gather(): pl.pallas_call(functools.partial(gather_kernel, dims), out_shape=(jax.Sha...  242 us
    pallas_call x1, Pallas kernels, finish(): pl.pallas_call(functools.partial(finish_kernel, roots), grid_spec=grid_sp...  75.7 us

profile of v1, /device:TPU:29, one launch (start us, length us, event | category | flops | bytes accessed | tf_op | source)
XLA Modules:
  0.0 328.7 jit_solution(7622895026997475902)
XLA Ops:
  0.0 0.6 pad_add_fusion.place
  0.6 0.7 constant_dynamic-slice_fusion.1
  1.3 1.2 slice_bitcast_fusion.head_pick
  2.5 0.7 constant_dynamic-slice_fusion
  3.2 1.3 slice.7
  4.5 1.3 dynamic_slice.11
  5.7 0.7 copy.8.col_pick
  6.4 0.7 copy.7.row_pick
  7.1 0.7 sqrt.3
  7.9 3.1 multiply_convert_fusion
  10.9 242.1 %gather.1 = (bf16[48,384,256]{2,1,0:T(8,128)(2,1)}, bf16[2,48,384,256]{3,2,1,0:T(8,128)(2,1)}, bf16[48,384,128]{2,1,0:T(8,128)(2,1)}) custom-call(bf16[12,384,256]{2,1,0:T(8,128)(2,1)} %bitcast.13), custom_call_target="tpu_custom_call" | custom-call | tf_op jit(solution)/shard_map/gather/pallas_call | solution.py:230
  253.0 75.7 %finish.1 = f32[1024,2048]{1,0:T(8,128)} custom-call(s32[4]{0:T(128)} %pad_add_fusion.place, s32[24,2]{1,0:T(8,128)} %copy.7.row_pick, s32[24,4]{1,0:T(8,128)} %copy.8.col_pick, s32[24]{0:T(128)} %slice_bitcast_fusion.head_pick, bf16[24,768,256]{2,1,0:T(8,128)(2,1)} %bitcast.14, bf16[2,24,768,256]{3,2,1,0:T(8,128)(2,1)} %bitcast.12, ...), custom_call_target="tpu_custom_call" | custom-call | tf_op jit(solution)/shard_map/finish/pallas_call | solution.py:468
